TPU v7x, 512 devices: a whole 4x4x16 slice. The times are simulated.
512 devices in a mesh: head: 8 (over x, core), tok: 64 (over z, y).
Axes of the slice: x: 4, y: 4, z: 16, core: 2. Of those that a mesh axis runs over, the one named last changes fastest.
Arguments:
- queries: bfloat16 [32768, 4096], P('tok', 'head'), may hold values from -16 to 16
- keys_fast: bfloat16 [32768, 4096], P('tok', 'head'), may hold values from -16 to 16
- values_fast: bfloat16 [32768, 4096], P('tok', 'head'), may hold values from -6 to 6
- keys_attn: bfloat16 [32768, 4096], P('tok', 'head'), may hold values from -16 to 16
- w_one: bfloat16 [8, 512, 256], P('head'), may hold values from -0.25 to 0.25
- w_three: bfloat16 [8, 512, 256], P('head'), may hold values from -0.25 to 0.25
- w_two: bfloat16 [8, 256, 512], P('head'), may hold values from -2 to 2
- step_size: float32 [8], P('head'), may hold values from 0.01 to 0.04
- norm_gain: float32 [4096], P('head'), may hold values from 0.25 to 1.75
- group_ids: int32 [32768], P('tok'), may hold values 0 or 1
- window_ids: int32 [32768], P('tok'), may hold values from 0 to 42, never falling along the last dimension, each value on 1 to 768 neighbouring positions
Outputs:
- mixed: bfloat16 [32768, 4096], P('tok', 'head')
Inputs may be any that keep to these rules, and one draw needn't show every extreme that they name: `window_ids`: window numbers never fall along the sequence and each number occurs; a window has 1 to 768 tokens, one exactly 768.
All inputs are finite; a program needn't handle non-finite values. No bound on the sum of `group_ids` on one device may be relied on, other than what follows from the above.
Results may differ from a plain program's by a relative error of at most 0.013.
Values may be sent and summed in bfloat16 or wider, within the bound.
A program may use at most 64 MiB of HBM per device.

v0:
```python
import math

import jax
import jax.numpy as jnp
from jax import lax
from jax.sharding import PartitionSpec as P

DH = 512
HEADS = 8
NBACK = 3


EPSILON = 1e-06


def shifted(block, axis, distance):
    devices = range(lax.axis_size(axis))
    route = [(i - distance, i) for i in devices if i - distance in devices]
    return lax.ppermute(block, axis, route)


def fast_grads(keys_rows, value_rows, group_mask, w_one, w_three, w_two):
    pre_one = jnp.einsum("thd,hdf->thf", keys_rows, w_one, preferred_element_type=jnp.float32)
    pre_three = jnp.einsum("thd,hdf->thf", keys_rows, w_three, preferred_element_type=jnp.float32)
    sigmoid_one = jax.nn.sigmoid(pre_one)
    hidden_act = (pre_one * sigmoid_one * pre_three * group_mask).astype(jnp.bfloat16)
    back_grad = jnp.einsum("thd,hfd->thf", value_rows, w_two, preferred_element_type=jnp.float32)
    delta_one = (
        -back_grad * pre_three * sigmoid_one * (1.0 + pre_one * (1.0 - sigmoid_one)) * group_mask
    ).astype(jnp.bfloat16)
    delta_three = (-back_grad * pre_one * sigmoid_one * group_mask).astype(jnp.bfloat16)
    grad_one = jnp.einsum("thd,thf->hdf", keys_rows, delta_one, preferred_element_type=jnp.float32)
    grad_three = jnp.einsum(
        "thd,thf->hdf", keys_rows, delta_three, preferred_element_type=jnp.float32
    )
    grad_two = -jnp.einsum(
        "thf,thd->hfd", hidden_act, value_rows, preferred_element_type=jnp.float32
    )
    return (grad_one, grad_three, grad_two)


def apply_step(weight, grad, sum_sq, count, rate):
    inverse = lax.rsqrt(sum_sq / count + EPSILON)
    return (
        weight.astype(jnp.float32) - rate[:, None, None] * grad * inverse[:, None, None]
    ).astype(jnp.bfloat16)


def fast_apply(query_rows, w_one, w_three, w_two):
    pre_one = jnp.einsum("thd,hdf->thf", query_rows, w_one, preferred_element_type=jnp.float32)
    pre_three = jnp.einsum("thd,hdf->thf", query_rows, w_three, preferred_element_type=jnp.float32)
    hidden_act = (pre_one * jax.nn.sigmoid(pre_one) * pre_three).astype(jnp.bfloat16)
    return jnp.einsum("thf,hfd->thd", hidden_act, w_two, preferred_element_type=jnp.float32)


def update_weights(weights, grads, rate):
    weight_one, weight_three, weight_two = weights
    grad_one, grad_three, grad_two = grads
    count = float(weight_one.shape[1] * weight_one.shape[2])
    grad_one, grad_three, grad_two = lax.psum((grad_one, grad_three, grad_two), "tok")
    return (
        apply_step(weight_one, grad_one, jnp.sum(grad_one * grad_one, axis=(1, 2)), count, rate),
        apply_step(
            weight_three, grad_three, jnp.sum(grad_three * grad_three, axis=(1, 2)), count, rate
        ),
        apply_step(weight_two, grad_two, jnp.sum(grad_two * grad_two, axis=(1, 2)), count, rate),
    )


def shards(
    queries,
    keys_fast,
    values_fast,
    keys_attn,
    w_one,
    w_three,
    w_two,
    step_size,
    norm_gain,
    group_ids,
    window_ids,
):
    tok_rows = queries.shape[0]
    local_heads = w_one.shape[0]
    head_size = w_one.shape[1]
    query_rows = queries.reshape(tok_rows, local_heads, head_size)
    keys_rows = keys_fast.reshape(tok_rows, local_heads, head_size)
    value_rows = values_fast.reshape(tok_rows, local_heads, head_size)
    attn_keys = keys_attn.reshape(tok_rows, local_heads, head_size)
    in_first = (group_ids == 0).astype(jnp.float32)[:, None, None]
    in_second = 1.0 - in_first
    weights = (w_one, w_three, w_two)
    outputs = []
    for group_mask in (in_first, in_second):
        grads = fast_grads(keys_rows, value_rows, group_mask, weights[0], weights[1], weights[2])
        weights = update_weights(weights, grads, step_size)
        outputs.append(fast_apply(query_rows, weights[0], weights[1], weights[2]))
    fast = jnp.where(in_first > 0.5, outputs[0], outputs[1])
    sum_sq = lax.psum(jnp.sum(fast * fast, axis=(1, 2)), "head")
    inverse = lax.rsqrt(sum_sq / (HEADS * DH) + EPSILON)
    values = (
        fast * inverse[:, None, None] * norm_gain.reshape(local_heads, head_size)[None, :, :]
    ).astype(jnp.bfloat16)
    window_marks = window_ids.astype(jnp.bfloat16)
    earlier = [
        shifted((attn_keys, values, window_marks), "tok", distance)
        for distance in range(NBACK, 0, -1)
    ]
    all_keys = jnp.concatenate([piece[0] for piece in earlier] + [attn_keys], axis=0)
    all_values = jnp.concatenate([piece[1] for piece in earlier] + [values], axis=0)
    key_window = jnp.concatenate([piece[2] for piece in earlier] + [window_marks], axis=0).astype(
        jnp.int32
    )
    position = lax.axis_index("tok")
    query_pos = position * tok_rows + jnp.arange(tok_rows, dtype=jnp.int32)
    key_pos = (
        position * tok_rows - NBACK * tok_rows + jnp.arange((NBACK + 1) * tok_rows, dtype=jnp.int32)
    )
    allowed = (
        (key_pos[None, :] <= query_pos[:, None])
        & (key_pos[None, :] >= 0)
        & (key_window[None, :] >= window_ids[:, None] - 1)
    )
    score_scale = 1.0 / math.sqrt(head_size)
    scores = (
        jnp.einsum("qhd,khd->hqk", query_rows, all_keys, preferred_element_type=jnp.float32)
        * score_scale
    )
    scores = jnp.where(allowed[None, :, :], scores, -1e30)
    row_max = jnp.max(scores, axis=2, keepdims=True)
    expo = jnp.where(allowed[None, :, :], jnp.exp(scores - row_max), 0.0)
    probs = (expo / jnp.sum(expo, axis=2, keepdims=True)).astype(jnp.bfloat16)
    mixed = jnp.einsum(
        "hqk,khd->qhd", probs, all_values, preferred_element_type=jnp.float32
    ).astype(jnp.bfloat16)
    return mixed.reshape(tok_rows, local_heads * head_size)


def solution(mesh):
    in_specs = (
        P("tok", "head"),
        P("tok", "head"),
        P("tok", "head"),
        P("tok", "head"),
        P("head", None, None),
        P("head", None, None),
        P("head", None, None),
        P("head"),
        P("head"),
        P("tok"),
        P("tok"),
    )
    out_specs = P("tok", "head")
    return jax.shard_map(shards, mesh=mesh, in_specs=in_specs, out_specs=out_specs, check_vma=False)
```

profile of v0, /device:TPU:80, one launch (start us, length us, event | category | flops | bytes accessed | tf_op | source)
XLA Modules:
  0.0 676.4 jit_solution(5391794296965640565)
XLA Ops:
  11.8 2.2 convolution_bitcast_fusion.9
  17.4 277.3 %all-reduce.7.cloned.1.call-done = (f32[1,512,256]{1,2,0:T(8,128)}, f32[1,256,512]{2,1,0:T(8,128)}, f32[1,512,256]{1,2,0:T(8,128)}) async-done(((f32[1,512,256]{1,2,0:T(8,128)}, f32[1,256,512]{2,1,0:T(8,128)}, f32[1,512,256]{1,2,0:T(8,128)}), (f32[1,512,256]{1,2,0:T(8,128)}, f32[1,256,512]{2,1,0:T(8,128)}, f32[1,512,256]{1,2,0:T(8,128)})) %all-reduce.7.cloned.1.call-update) | async-done | bytes 1572880 | tf_op jit(solution)/shard_map/psum | solution.py:60
  294.7 1.8 multiply_reduce_fusion.4
  297.2 1.8 multiply_reduce_fusion.6
  299.7 1.8 multiply_reduce_fusion.5
  308.2 3.1 collective-permute-start.5
  311.3 4.7 collective-permute-start.4
  316.0 3.8 collective-permute-start.3
  319.8 2.1 collective-permute-start.8
  321.9 4.7 collective-permute-start.7
  326.7 4.3 collective-permute-start.6
  331.4 253.2 %all-reduce.5.cloned.1.call-done = (f32[1,512,256]{1,2,0:T(8,128)}, f32[1,256,512]{2,1,0:T(8,128)}, f32[1,512,256]{1,2,0:T(8,128)}) async-done(((f32[1,512,256]{1,2,0:T(8,128)}, f32[1,256,512]{2,1,0:T(8,128)}, f32[1,512,256]{1,2,0:T(8,128)}), (f32[1,512,256]{1,2,0:T(8,128)}, f32[1,256,512]{2,1,0:T(8,128)}, f32[1,512,256]{1,2,0:T(8,128)})) %all-reduce.5.cloned.1.call-update) | async-done | bytes 1572880 | tf_op jit(solution)/shard_map/psum | solution.py:60
  593.4 2.9 convolution_bitcast_fusion
  596.3 1.9 multiply_reduce_fusion
  598.2 12.4 %psum.55 = f32[512]{0:T(512)S(1)} all-reduce(f32[512]{0:T(512)S(1)} %get-tuple-element.17), channel_id=1, replica_groups=mesh['head'=8,'tok'=64] {'head'}, use_global_device_ids=true, to_apply=%region_13.14 | all-reduce | flops 512 | bytes 4096 | tf_op jit(solution)/shard_map/psum | solution.py:99
  610.8 3.1 collective-permute-start.2
  613.8 4.7 collective-permute-start.1
  618.6 3.8 collective-permute-start
  622.4 6.1 fusion
  628.4 2.4 fusion.1
  630.9 4.0 collective-permute-done.2
  634.9 2.9 collective-permute-done.1
  637.9 28.1 %collective-permute-done = bf16[512,1,512]{0,2,1:T(8,128)(2,1)S(1)} collective-permute-done((bf16[512,1,512]{0,2,1:T(8,128)(2,1)S(1)}, bf16[512,1,512]{0,2,1:T(8,128)(2,1)S(1)}, u32[]{:S(2)}, u32[]{:S(2)}) %collective-permute-start) | collective-permute-done | bytes 524320 | tf_op jit(solution)/shard_map/ppermute | solution.py:19
  666.0 2.5 fusion.24
  (60 shorter events, 22.2 us)
Async XLA Ops:
  6.5 324.5 %copy-start = (bf16[512,512]{1,0:T(8,128)(2,1)S(1)}, bf16[512,512]{1,0:T(8,128)(2,1)}, u32[]{:S(2)}) copy-start(bf16[512,512]{1,0:T(8,128)(2,1)} %param.11) | copy-start | bytes 1572868
  6.5 7.4 %copy-start.1 = (bf16[512,512]{1,0:T(8,128)(2,1)S(1)}, bf16[512,512]{1,0:T(8,128)(2,1)}, u32[]{:S(2)}) copy-start(bf16[512,512]{1,0:T(8,128)(2,1)} %param.12) | copy-start | bytes 1572868
  6.5 288.1 %all-reduce.7.cloned.1.call-start = ((), (), s32[]{:S(2)}) async-start(), calls=%async_computation.1 | async-start | bytes 3145728 | tf_op jit(solution)/shard_map/psum | solution.py:60
  10.3 4.9 copy-start.3
  14.0 2.4 copy-start.5
  14.0 2.6 copy-start.6
  14.0 3.4 copy-start.7
  16.3 287.6 %copy-start.4 = (bf16[1,256,512]{2,1,0:T(8,128)(2,1)S(1)}, bf16[1,256,512]{2,1,0:T(8,128)(2,1)}, u32[]{:S(2)}) copy-start(bf16[1,256,512]{2,1,0:T(8,128)(2,1)} %param.17) | copy-start | bytes 786436
  16.4 568.3 %all-reduce.5.cloned.1.call-start = ((), (), s32[]{:S(2)}) async-start(), calls=%async_computation | async-start | bytes 3145728 | tf_op jit(solution)/shard_map/psum | solution.py:60
  294.7 9.2 %copy-start.2 = (f32[1,256,512]{2,1,0:T(8,128)S(1)}, f32[1,256,512]{2,1,0:T(8,128)}, u32[]{:S(2)}) copy-start(f32[1,256,512]{2,1,0:T(8,128)} %get-tuple-element.9) | copy-start | bytes 1572868
  305.8 2.4 copy-start.9
  308.2 18.4 %collective-permute-start.5 = (bf16[512]{0:T(512)(128)(2,1)S(1)}, bf16[512]{0:T(512)(128)(2,1)S(1)}, u32[]{:S(2)}, u32[]{:S(2)}) collective-permute-start(bf16[512]{0:T(512)(128)(2,1)S(1)} %get-tuple-element.13), channel_id=1, source_target_pairs={{0,1},{1,2},{2,3},{3,4},{4,5},{5,6},{6,7},{7,8},{8,9},{9,10},{10,1... | collective-permute-start | bytes 3080 | tf_op jit(solution)/shard_map/ppermute | solution.py:19
  311.3 19.7 %collective-permute-start.4 = (bf16[512]{0:T(512)(128)(2,1)S(1)}, bf16[512]{0:T(512)(128)(2,1)S(1)}, u32[]{:S(2)}, u32[]{:S(2)}) collective-permute-start(bf16[512]{0:T(512)(128)(2,1)S(1)} %get-tuple-element.13), channel_id=1, source_target_pairs={{0,2},{1,3},{2,4},{3,5},{4,6},{5,7},{6,8},{7,9},{8,10},{9,11},{10,... | collective-permute-start | bytes 3080 | tf_op jit(solution)/shard_map/ppermute | solution.py:19
  316.0 15.0 %collective-permute-start.3 = (bf16[512]{0:T(512)(128)(2,1)S(1)}, bf16[512]{0:T(512)(128)(2,1)S(1)}, u32[]{:S(2)}, u32[]{:S(2)}) collective-permute-start(bf16[512]{0:T(512)(128)(2,1)S(1)} %get-tuple-element.13), channel_id=1, source_target_pairs={{0,3},{1,4},{2,5},{3,6},{4,7},{5,8},{6,9},{7,10},{8,11},{9,12},{10... | collective-permute-start | bytes 3080 | tf_op jit(solution)/shard_map/ppermute | solution.py:19
  319.8 298.7 %collective-permute-start.8 = (bf16[512,1,512]{2,0,1:T(8,128)(2,1)}, bf16[512,1,512]{2,0,1:T(8,128)(2,1)}, u32[]{:S(2)}, u32[]{:S(2)}) collective-permute-start(bf16[512,1,512]{2,0,1:T(8,128)(2,1)} %bitcast.60), channel_id=1, source_target_pairs={{0,1},{1,2},{2,3},{3,4},{4,5},{5,6},{6,7},{7,8},{8,9},{9,10},{10,1... | collective-permute-start | bytes 1572872 | tf_op jit(solution)/shard_map/ppermute | solution.py:19
  321.9 300.5 %collective-permute-start.7 = (bf16[512,1,512]{2,0,1:T(8,128)(2,1)}, bf16[512,1,512]{2,0,1:T(8,128)(2,1)}, u32[]{:S(2)}, u32[]{:S(2)}) collective-permute-start(bf16[512,1,512]{2,0,1:T(8,128)(2,1)} %bitcast.60), channel_id=1, source_target_pairs={{0,2},{1,3},{2,4},{3,5},{4,6},{5,7},{6,8},{7,9},{8,10},{9,11},{10,... | collective-permute-start | bytes 1572872 | tf_op jit(solution)/shard_map/ppermute | solution.py:19
  326.7 295.7 %collective-permute-start.6 = (bf16[512,1,512]{2,0,1:T(8,128)(2,1)}, bf16[512,1,512]{2,0,1:T(8,128)(2,1)}, u32[]{:S(2)}, u32[]{:S(2)}) collective-permute-start(bf16[512,1,512]{2,0,1:T(8,128)(2,1)} %bitcast.60), channel_id=1, source_target_pairs={{0,3},{1,4},{2,5},{3,6},{4,7},{5,8},{6,9},{7,10},{8,11},{9,12},{10... | collective-permute-start | bytes 1572872 | tf_op jit(solution)/shard_map/ppermute | solution.py:19
  593.4 17.1 %copy-start.8 = (f32[512]{0:T(512)S(1)}, f32[512]{0:T(512)}, u32[]{:S(2)}) copy-start(f32[512]{0:T(512)} %param.19) | copy-start | bytes 6148
  610.8 24.2 %collective-permute-start.2 = (bf16[512,1,512]{0,2,1:T(8,128)(2,1)S(1)}, bf16[512,1,512]{0,2,1:T(8,128)(2,1)S(1)}, u32[]{:S(2)}, u32[]{:S(2)}) collective-permute-start(bf16[512,1,512]{0,2,1:T(8,128)(2,1)S(1)} %fusion.29), channel_id=1, source_target_pairs={{0,1},{1,2},{2,3},{3,4},{4,5},{5,6},{6,7},{7,8},{8,9},{9,10},{10,1... | collective-permute-start | bytes 1572872 | tf_op jit(solution)/shard_map/ppermute | solution.py:19
  613.8 24.0 %collective-permute-start.1 = (bf16[512,1,512]{0,2,1:T(8,128)(2,1)S(1)}, bf16[512,1,512]{0,2,1:T(8,128)(2,1)S(1)}, u32[]{:S(2)}, u32[]{:S(2)}) collective-permute-start(bf16[512,1,512]{0,2,1:T(8,128)(2,1)S(1)} %fusion.29), channel_id=1, source_target_pairs={{0,2},{1,3},{2,4},{3,5},{4,6},{5,7},{6,8},{7,9},{8,10},{9,11},{10,... | collective-permute-start | bytes 1572872 | tf_op jit(solution)/shard_map/ppermute | solution.py:19
  618.6 47.5 %collective-permute-start = (bf16[512,1,512]{0,2,1:T(8,128)(2,1)S(1)}, bf16[512,1,512]{0,2,1:T(8,128)(2,1)S(1)}, u32[]{:S(2)}, u32[]{:S(2)}) collective-permute-start(bf16[512,1,512]{0,2,1:T(8,128)(2,1)S(1)} %fusion.29), channel_id=1, source_target_pairs={{0,3},{1,4},{2,5},{3,6},{4,7},{5,8},{6,9},{7,10},{8,11},{9,12},{10... | collective-permute-start | bytes 1572872 | tf_op jit(solution)/shard_map/ppermute | solution.py:19
Sparse Core Ops, SparseCore 0:
  16.5 278.1 all-reduce.6
  308.3 276.2 all-reduce.4
where the time goes:
time: 677 us; the launch traced here: 676 us
  waiting for transfers between devices  566 us (84%)
  starting transfers between devices  34.3 us (5%)
  matrix products  28.5 us (4%)
  between operations  18.6 us (3%)
  other arithmetic  15.7 us (2%)
  blocking collectives  12.4 us (2%)
    psum x2, waiting for transfers between devices, update_weights(): lax.psum((grad_one, grad_three, grad_two), 'tok')  531 us
    ppermute x9, waiting for transfers between devices, shifted(): return lax.ppermute(block, axis, route)  35.1 us
    ppermute x9, starting transfers between devices, shifted(): return lax.ppermute(block, axis, route)  34.2 us
  transfers between devices with their start and end apart: 11, of which 5 were waited for; matrix products, arithmetic and copies ran while one was open for 3% of the time, Pallas kernels for 0%

commit v1 on v0

v1 whole, which is shorter than its diff:
```python
import functools
import math

import jax
import jax.numpy as jnp
from jax import lax
from jax.experimental import pallas as pl
from jax.experimental.pallas import tpu as pltpu
from jax.sharding import PartitionSpec as P

NY = 4
NCORE = 2
NBACK = 3
EPSILON = 1e-06
MESH = pl.DeviceIdType.MESH
F32 = jnp.float32
BF16 = jnp.bfloat16


def dot_nt(a, b):
    return lax.dot_general(a, b, (((1,), (1,)), ((), ())), preferred_element_type=F32)


def dot_nn(a, b):
    return lax.dot_general(a, b, (((1,), (0,)), ((), ())), preferred_element_type=F32)


def sigmoid(x):
    return 0.5 * jnp.tanh(0.5 * x) + 0.5


def aligned(index, step):
    return pl.ds(pl.multiple_of(index * step, step), step)


def kernel(
    dims,
    k_ref,
    v_ref,
    w1_ref,
    w3_ref,
    w2_ref,
    rate_ref,
    gain_ref,
    gid_ref,
    wid_ref,
    q_hbm,
    a_hbm,
    out_ref,
    qall,
    aall,
    ids,
    pre,
    back,
    delta,
    grad_send,
    grad_own,
    y_in,
    z_out,
    z_own,
    z_in,
    gathered,
    weights,
    w2t,
    scores,
    probs,
    hidden,
    fast,
    values,
    sq_in,
    local_sem,
    y_send,
    y_recv,
    z_send,
    z_recv,
    zg_send,
    zg_recv,
    yg_send,
    yg_recv,
    halo_send,
    halo_recv,
    head_send,
    head_recv,
):
    nz, nhead, rows, dh, hid = dims
    ntok = nz * NY
    cols = dh // 128
    head_rows = 2 * hid // NY
    tail_rows = hid // NY
    piece = head_rows + tail_rows
    block = piece * cols // nz
    t = lax.axis_index("tok")
    h = lax.axis_index("head")
    z = lax.div(t, NY)
    y = lax.rem(t, NY)

    def y_peer(d):
        return z * NY + lax.rem(y + d, NY)

    def z_peer(d):
        return lax.rem(z + d, nz) * NY + y

    def remote(src, dst, send, recv, **where):
        return pltpu.make_async_remote_copy(
            src_ref=src, dst_ref=dst, send_sem=send, recv_sem=recv, device_id=where, device_id_type=MESH
        )

    load_a = pltpu.make_async_copy(a_hbm, aall.at[NBACK], local_sem.at[0])
    load_q = pltpu.make_async_copy(q_hbm, qall.at[NBACK], local_sem.at[1])
    load_a.start()
    load_q.start()

    barrier = pltpu.get_barrier_semaphore()

    def greet(**where):
        pl.semaphore_signal(barrier, inc=1, device_id=where, device_id_type=MESH)

    for d in range(1, NY):
        greet(tok=y_peer(d))

    @pl.loop(1, nz)
    def _(d):
        greet(tok=z_peer(d))

    for d in range(1, NBACK + 1):
        greet(tok=lax.rem(t + ntok - d, ntok))
    for d in range(1, nhead):
        greet(head=lax.rem(h + d, nhead))

    ids[NBACK, 0:1, :] = wid_ref[...].reshape(1, rows)
    ids[NBACK, 1:2, :] = gid_ref[...].reshape(1, rows)
    weights[0, 0:hid, :] = w1_ref[0].T
    weights[0, hid : 2 * hid, :] = w3_ref[0].T
    weights[0, 2 * hid : 3 * hid, :] = w2_ref[0]

    def y_scatter(r, d):
        p = lax.rem(y + d, NY)
        return remote(
            grad_send.at[r, p], y_in.at[r, d - 1], y_send.at[r, d - 1], y_recv.at[r, d - 1], tok=y_peer(d)
        )

    def z_scatter(r, d):
        n = lax.rem(z + d, nz)
        return remote(
            z_out.at[r, aligned(n, block)],
            z_in.at[r, d - 1],
            z_send.at[r, d - 1],
            z_recv.at[r, d - 1],
            tok=z_peer(d),
        )

    def z_gather(r, d, owner):
        part = gathered.at[r, y, aligned(owner, block)]
        return remote(part, part, zg_send.at[r, d - 1], zg_recv.at[r, d - 1], tok=z_peer(d))

    def y_gather(r, d, owner):
        part = gathered.at[r, owner]
        return remote(part, part, yg_send.at[r, d - 1], yg_recv.at[r, d - 1], tok=y_peer(d))

    def halo(which, d):
        buffer = (aall, qall, ids)[which]
        return remote(
            buffer.at[NBACK],
            buffer.at[NBACK - d],
            halo_send.at[which, d - 1],
            halo_recv.at[which, d - 1],
            tok=lax.rem(t + d, ntok),
        )

    def head_share(d):
        return remote(
            sq_in.at[0], sq_in.at[d], head_send.at[d - 1], head_recv.at[d - 1], head=lax.rem(h + d, nhead)
        )

    def gradients(r):
        pre[...] = dot_nt(weights[r, 0 : 2 * hid, :], k_ref[...])
        back[0:hid, :] = dot_nt(weights[r, 2 * hid : 3 * hid, :], v_ref[...])
        mask = (ids[NBACK, 1:2, :] == r).astype(F32)

        @pl.loop(0, hid // 32)
        def _(i):
            p1 = pre[aligned(i, 32), :]
            p3 = pre[pl.ds(pl.multiple_of(hid + i * 32, 32), 32), :]
            b = back[aligned(i, 32), :] * mask
            s1 = sigmoid(p1)
            silu = p1 * s1
            delta[aligned(i, 32), :] = (-b * p3 * s1 * (1.0 + p1 * (1.0 - s1))).astype(BF16)
            delta[pl.ds(pl.multiple_of(hid + i * 32, 32), 32), :] = (-b * silu).astype(BF16)
            delta[pl.ds(pl.multiple_of(2 * hid + i * 32, 32), 32), :] = (-silu * p3 * mask).astype(BF16)

        for d in (1, 2, 3, 0):
            p = lax.rem(y + d, NY)
            upper = dot_nn(delta[aligned(p, head_rows), :], k_ref[...])
            lower = dot_nn(
                delta[pl.ds(pl.multiple_of(2 * hid + p * tail_rows, tail_rows), tail_rows), :], v_ref[...]
            )
            for j in range(cols):
                top = slice(j * piece, j * piece + head_rows)
                bottom = slice(j * piece + head_rows, (j + 1) * piece)
                lanes = slice(j * 128, (j + 1) * 128)
                if d:
                    grad_send[r, p, top, :] = upper[:, lanes].astype(BF16)
                    grad_send[r, p, bottom, :] = lower[:, lanes].astype(BF16)
                else:
                    grad_own[top, :] = upper[:, lanes]
                    grad_own[bottom, :] = lower[:, lanes]
            if d:
                if r == 0 and d == 1:
                    pl.semaphore_wait(barrier, (NY - 1) + (nz - 1) + NBACK + (nhead - 1))
                y_scatter(r, d).start()

    def scatter_z(r):
        for d in range(1, NY):
            y_scatter(r, d).wait_recv()

        def total(n):
            own = grad_own[aligned(n, block), :]
            for d in range(1, NY):
                own = own + y_in[r, d - 1, aligned(n, block), :].astype(F32)
            return own

        @pl.loop(1, nz)
        def _(d):
            n = lax.rem(z + d, nz)
            z_out[r, aligned(n, block), :] = total(n).astype(BF16)
            z_scatter(r, d).start()

        z_own[...] = total(z)

    def gather_z(r):
        def add(d, total):
            z_scatter(r, d).wait_recv()
            return total + z_in[r, d - 1].astype(F32)

        total = lax.fori_loop(1, nz, add, z_own[...])
        gathered[r, y, aligned(z, block), :] = total.astype(BF16)

        @pl.loop(1, nz)
        def _(d):
            z_gather(r, d, z).start()

    def gather_y(r):
        @pl.loop(1, nz)
        def _(d):
            z_gather(r, d, lax.rem(z + nz - d, nz)).wait_recv()

        for d in range(1, NY):
            y_gather(r, d, y).start()

    def finish_y(r):
        for d in range(1, NY):
            y_gather(r, d, lax.rem(y + NY - d, NY)).wait_recv()

    def update(r):
        def squares(x):
            x = x.astype(F32)
            return jnp.sum((x * x).reshape(-1, 8, 128), axis=0)

        sums = [jnp.zeros((8, 128), F32) for _ in range(3)]
        for p in range(NY):
            for j in range(cols):
                which = p // (NY // 2)
                sums[which] = sums[which] + squares(gathered[r, p, j * piece : j * piece + head_rows, :])
                sums[2] = sums[2] + squares(gathered[r, p, j * piece + head_rows : (j + 1) * piece, :])
        scale = [
            rate_ref[...] * lax.rsqrt(jnp.sum(s, axis=(0, 1), keepdims=True) / float(hid * dh) + EPSILON)
            for s in sums
        ]
        for p in range(NY):
            for j in range(cols):
                lanes = slice(j * 128, (j + 1) * 128)
                top = slice(p * head_rows, (p + 1) * head_rows)
                bottom = slice(2 * hid + p * tail_rows, 2 * hid + (p + 1) * tail_rows)
                upper = gathered[r, p, j * piece : j * piece + head_rows, :].astype(F32)
                lower = gathered[r, p, j * piece + head_rows : (j + 1) * piece, :].astype(F32)
                weights[r + 1, top, lanes] = (
                    weights[r, top, lanes].astype(F32) - upper * scale[p // (NY // 2)]
                ).astype(BF16)
                weights[r + 1, bottom, lanes] = (
                    weights[r, bottom, lanes].astype(F32) - lower * scale[2]
                ).astype(BF16)

    def attend():
        for which in (0, 2):
            for d in range(1, NBACK + 1):
                halo(which, d).wait_recv()

        @pl.loop(0, NBACK + 1)
        def _(s):
            scores[s] = dot_nt(qall[NBACK], aall[s])

        mark = jnp.broadcast_to(ids[NBACK, 0:1, :].astype(F32), (128, rows)).T
        back[0:rows, 0:128] = mark

        @pl.loop(0, rows // 16)
        def _(i):
            here = aligned(i, 16)
            query_mark = back[here, 0:1] - 1.0
            query_at = t * rows + i * 16 + lax.broadcasted_iota(jnp.int32, (16, rows), 0)
            parts = []
            for s in range(NBACK + 1):
                key_at = (t - NBACK + s) * rows + lax.broadcasted_iota(jnp.int32, (16, rows), 1)
                allowed = (
                    (key_at <= query_at) & (key_at >= 0) & (ids[s, 0:1, :].astype(F32) >= query_mark)
                )
                parts.append(jnp.where(allowed, scores[s, here, :] * (1.0 / math.sqrt(dh)), -1e30))
            top = parts[0]
            for part in parts[1:]:
                top = jnp.maximum(top, part)
            top = jnp.max(top, axis=1, keepdims=True)
            parts = [jnp.exp(part - top) for part in parts]
            whole = parts[0]
            for part in parts[1:]:
                whole = whole + part
            inverse = 1.0 / jnp.sum(whole, axis=1, keepdims=True)
            for s in range(NBACK + 1):
                probs[s, here, :] = (parts[s] * inverse).astype(BF16)

    def apply_fast(r):
        w2t[...] = weights[r + 1, 2 * hid : 3 * hid, :].T

        @pl.loop(0, NBACK + 1)
        def _(s):
            pre[...] = dot_nt(weights[r + 1, 0 : 2 * hid, :], qall[s])

            @pl.loop(0, hid // 32)
            def _(i):
                p1 = pre[aligned(i, 32), :]
                p3 = pre[pl.ds(pl.multiple_of(hid + i * 32, 32), 32), :]
                hidden[aligned(i, 32), :] = (p1 * sigmoid(p1) * p3).astype(BF16)

            if r == 0:
                fast[s] = dot_nn(w2t[...], hidden[...])
            else:
                pre[...] = dot_nn(w2t[...], hidden[...])
                first = ids[s, 1:2, :] == 0

                def select(i, total):
                    here = aligned(i, 32)
                    mixed = jnp.where(first, fast[s, here, :], pre[here, :])
                    fast[s, here, :] = mixed
                    return total + jnp.sum((mixed * mixed).reshape(4, 8, rows), axis=0)

                total = lax.fori_loop(0, dh // 32, select, jnp.zeros((8, rows), F32))
                total = jnp.sum(total, axis=0, keepdims=True)
                for j in range(rows // 128):
                    sq_in[0, s, j : j + 1, :] = total[:, j * 128 : (j + 1) * 128]

    gradients(0)
    scatter_z(0)
    load_a.wait()
    for d in range(1, NBACK + 1):
        halo(2, d).start()
        halo(0, d).start()
    gather_z(0)
    gather_y(0)
    load_q.wait()
    finish_y(0)
    update(0)
    gradients(1)
    scatter_z(1)
    for d in range(1, NBACK + 1):
        halo(1, d).start()
    attend()
    gather_z(1)
    gather_y(1)
    for d in range(1, NBACK + 1):
        halo(1, d).wait_recv()
    apply_fast(0)
    finish_y(1)
    update(1)
    apply_fast(1)
    for d in range(1, nhead):
        head_share(d).start()
    for d in range(1, nhead):
        head_share(d).wait_recv()

    for s in range(NBACK + 1):
        total = sq_in[0, s]
        for d in range(1, nhead):
            total = total + sq_in[d, s]
        inverse = lax.rsqrt(total / float(nhead * dh) + EPSILON)
        inverse = jnp.concatenate([inverse[j : j + 1, :] for j in range(rows // 128)], axis=1)

        @pl.loop(0, dh // 32)
        def _(i):
            here = aligned(i, 32)
            values[here, s * rows : (s + 1) * rows] = (fast[s, here, :] * inverse).astype(BF16)

    for s in range(NBACK + 1):
        product = dot_nt(probs[s], values[:, s * rows : (s + 1) * rows])
        pre[...] = product if s == 0 else pre[...] + product
    out_ref[...] = (pre[...] * gain_ref[...].reshape(1, dh)).astype(BF16)

    for r in range(2):
        for d in range(1, NY):
            y_scatter(r, d).wait_send()
            y_gather(r, d, y).wait_send()

        @pl.loop(1, nz)
        def _(d):
            z_scatter(r, d).wait_send()
            z_gather(r, d, z).wait_send()

    for which in range(3):
        for d in range(1, NBACK + 1):
            halo(which, d).wait_send()
    for d in range(1, nhead):
        head_share(d).wait_send()


def shards(queries, keys_fast, values_fast, keys_attn, w_one, w_three, w_two, step_size, norm_gain, group_ids, window_ids):
    rows, dh = queries.shape
    hid = w_one.shape[2]
    nz = lax.axis_size("tok") // NY
    nhead = lax.axis_size("head")
    piece = 3 * hid // NY * (dh // 128)
    block = piece // nz
    dma = pltpu.SemaphoreType.DMA
    vmem = pl.BlockSpec(memory_space=pltpu.VMEM)
    anywhere = pl.BlockSpec(memory_space=pl.ANY)
    return pl.pallas_call(
        functools.partial(kernel, (nz, nhead, rows, dh, hid)),
        out_shape=jax.ShapeDtypeStruct((rows, dh), BF16),
        in_specs=[vmem] * 9 + [anywhere] * 2,
        out_specs=vmem,
        scratch_shapes=[
            pltpu.VMEM((NBACK + 1, rows, dh), BF16),
            pltpu.VMEM((NBACK + 1, rows, dh), BF16),
            pltpu.VMEM((NBACK + 1, 8, rows), jnp.int32),
            pltpu.VMEM((2 * hid, rows), F32),
            pltpu.VMEM((max(hid, rows), rows), F32),
            pltpu.VMEM((3 * hid, rows), BF16),
            pltpu.VMEM((2, NY, piece, 128), BF16),
            pltpu.VMEM((piece, 128), F32),
            pltpu.VMEM((2, NY - 1, piece, 128), BF16),
            pltpu.VMEM((2, piece, 128), BF16),
            pltpu.VMEM((block, 128), F32),
            pltpu.VMEM((2, nz - 1, block, 128), BF16),
            pltpu.VMEM((2, NY, piece, 128), BF16),
            pltpu.VMEM((3, 3 * hid, dh), BF16),
            pltpu.VMEM((dh, hid), BF16),
            pltpu.VMEM((NBACK + 1, rows, rows), F32),
            pltpu.VMEM((NBACK + 1, rows, rows), BF16),
            pltpu.VMEM((hid, rows), BF16),
            pltpu.VMEM((NBACK + 1, dh, rows), F32),
            pltpu.VMEM((dh, (NBACK + 1) * rows), BF16),
            pltpu.VMEM((nhead, NBACK + 1, rows // 128, 128), F32),
            dma((2,)),
            dma((2, NY - 1)),
            dma((2, NY - 1)),
            dma((2, nz - 1)),
            dma((2, nz - 1)),
            dma((2, nz - 1)),
            dma((2, nz - 1)),
            dma((2, NY - 1)),
            dma((2, NY - 1)),
            dma((3, NBACK)),
            dma((3, NBACK)),
            dma((nhead - 1,)),
            dma((nhead - 1,)),
        ],
        compiler_params=pltpu.CompilerParams(
            collective_id=0, has_side_effects=True, vmem_limit_bytes=56 * 1024 * 1024
        ),
        name="fast_weight_attention",
    )(
        keys_fast,
        values_fast,
        w_one,
        w_three,
        w_two,
        step_size.reshape(1, 1),
        norm_gain,
        group_ids,
        window_ids,
        queries,
        keys_attn,
    )


def solution(mesh):
    in_specs = (
        P("tok", "head"),
        P("tok", "head"),
        P("tok", "head"),
        P("tok", "head"),
        P("head", None, None),
        P("head", None, None),
        P("head", None, None),
        P("head"),
        P("head"),
        P("tok"),
        P("tok"),
    )
    return jax.shard_map(shards, mesh=mesh, in_specs=in_specs, out_specs=P("tok", "head"), check_vma=False)
```

time: 677 us -> 206 us (0.30)
  the two profiles are of different devices: /device:TPU:80 before, /device:TPU:6 now
where the time goes in v1:
time: 206 us; the launch traced here: 204 us
  Pallas kernels  202 us (98%)
    pallas_call x1, Pallas kernels, shards(): pl.pallas_call(functools.partial(kernel, (nz, nhead, rows, dh, hid)), out...  202 us

profile of v1, /device:TPU:6, one launch (start us, length us, event | category | flops | bytes accessed | tf_op | source)
XLA Modules:
  0.0 204.3 jit_solution(13806014929073523236)
XLA Ops:
  0.7 201.8 %fast_weight_attention.1 = bf16[512,512]{1,0:T(8,128)(2,1)} custom-call(bf16[512,512]{1,0:T(8,128)(2,1)} %k_ref.1, bf16[512,512]{1,0:T(8,128)(2,1)} %v_ref.1, bf16[1,512,256]{2,1,0:T(8,128)(2,1)} %w1_ref.1, bf16[1,512,256]{2,1,0:T(8,128)(2,1)} %w3_ref.1, bf16[1,256,512]{2,1,0:T(8,128)(2,1)} %w2_ref.1, f32[1,1]{1,0:T(1,128)} %bitcast.1.rate_ref, ...), custom_call_target="tpu_custom_call" | custom-call | tf_op jit(solution)/shard_map/fast_weight_attention/pallas_call | solution.py:422
  202.5 1.9 copy.14

commit v2 on v1

v2 whole, which is shorter than its diff:
```python
import functools
import math

import jax
import jax.numpy as jnp
from jax import lax
from jax.experimental import pallas as pl
from jax.experimental.pallas import tpu as pltpu
from jax.sharding import PartitionSpec as P

NY = 4
NCORE = 2
NBACK = 3
KEY_PARTS = 8
EPSILON = 1e-06
MESH = pl.DeviceIdType.MESH
F32 = jnp.float32
BF16 = jnp.bfloat16


def dot_nt(a, b):
    return lax.dot_general(a, b, (((1,), (1,)), ((), ())), preferred_element_type=F32)


def dot_nn(a, b):
    return lax.dot_general(a, b, (((1,), (0,)), ((), ())), preferred_element_type=F32)


def sigmoid(x):
    return 0.5 * jnp.tanh(0.5 * x) + 0.5


def aligned(index, step):
    return pl.ds(pl.multiple_of(index * step, step), step)


def kernel(
    dims,
    k_ref,
    v_ref,
    w1_ref,
    w3_ref,
    w2_ref,
    rate_ref,
    gain_ref,
    gid_ref,
    wid_ref,
    q_ref,
    a_hbm,
    out_ref,
    aall,
    ids,
    pre,
    back,
    delta,
    weights,
    w2t,
    scores,
    probs,
    hidden_first,
    hidden,
    fast,
    norms,
    sq_in,
    local_sem,
    halo_sems,
    head_sems,
    key_sems,
    *chunks,
):
    nz, nhead, rows, dh, hid = dims
    ntok = nz * NY
    cols = dh // 128
    t = lax.axis_index("tok")
    h = lax.axis_index("head")
    z = lax.div(t, NY)
    y = lax.rem(t, NY)
    starts = (0, 2 * hid)
    heights = (2 * hid // NY, hid // NY)
    pieces = tuple(height * cols for height in heights)
    blocks = tuple(piece // nz for piece in pieces)

    def y_peer(d):
        return z * NY + lax.rem(y + d, NY)

    def z_peer(d):
        return lax.rem(z + d, nz) * NY + y

    def remote(src, dst, sems, index, **where):
        return pltpu.make_async_remote_copy(
            src_ref=src,
            dst_ref=dst,
            send_sem=sems.at[(0, *index)],
            recv_sem=sems.at[(1, *index)],
            device_id=where,
            device_id_type=MESH,
        )

    load_a = pltpu.make_async_copy(a_hbm, aall.at[NBACK], local_sem)
    load_a.start()

    barrier = pltpu.get_barrier_semaphore()

    def greet(**where):
        pl.semaphore_signal(barrier, inc=1, device_id=where, device_id_type=MESH)

    @pl.loop(1, nz)
    def _(d):
        greet(tok=z_peer(d))

    for d in range(1, NY):
        greet(tok=y_peer(d))
    for d in range(1, NBACK + 1):
        greet(tok=lax.rem(t + ntok - d, ntok))
    for d in range(1, nhead):
        greet(head=lax.rem(h + d, nhead))

    ids[NBACK, 0:1, :] = wid_ref[...].reshape(1, rows)
    ids[NBACK, 1:2, :] = gid_ref[...].reshape(1, rows)
    weights[0, 0:hid, :] = w1_ref[0].T
    weights[0, hid : 2 * hid, :] = w3_ref[0].T
    weights[0, 2 * hid : 3 * hid, :] = w2_ref[0]

    def y_scatter(r, c, d):
        grad_send, y_in, sems = chunks[c][0], chunks[c][1], chunks[c][7]
        return remote(
            grad_send.at[r, lax.rem(y + d, NY)], y_in.at[r, d - 1], sems, (r, d - 1), tok=y_peer(d)
        )

    def z_scatter(r, c, d):
        z_out, z_in, sems = chunks[c][3], chunks[c][5], chunks[c][8]
        n = lax.rem(z + d, nz)
        return remote(
            z_out.at[r, aligned(n, blocks[c])], z_in.at[r, d - 1], sems, (r, d - 1), tok=z_peer(d)
        )

    def z_gather(r, c, d, owner):
        part = chunks[c][6].at[r, y, aligned(owner, blocks[c])]
        return remote(part, part, chunks[c][9], (r, d - 1), tok=z_peer(d))

    def y_gather(r, c, d, owner):
        part = chunks[c][6].at[r, owner]
        return remote(part, part, chunks[c][10], (r, d - 1), tok=y_peer(d))

    def key_piece(n):
        d = (1, 3, 2)[n % NBACK]
        part = n // NBACK
        here = slice(part * rows // KEY_PARTS, (part + 1) * rows // KEY_PARTS)
        return remote(
            aall.at[NBACK, here],
            aall.at[NBACK - d, here],
            key_sems,
            (d - 1, part),
            tok=lax.rem(t + d, ntok),
        )

    def reaches(shard, n):
        left = lax.rem(shard, 3)
        return left != 0 if n // NBACK >= KEY_PARTS // 2 else left == 1

    def send_keys(first, last):
        for n in range(first, last):
            if n % NBACK == 1:

                @pl.when(reaches(lax.rem(t + NBACK, ntok), n))
                def _():
                    key_piece(n).start()
            else:
                key_piece(n).start()

    def wait_keys(sent):
        for n in range(NBACK * KEY_PARTS):
            wait = key_piece(n).wait_send if sent else key_piece(n).wait_recv
            if n % NBACK == 1:
                pl.when(reaches(lax.rem(t + NBACK, ntok) if sent else t, n))(wait)
            else:
                wait()

    def halo(which, d):
        buffer = (ids, hidden, norms)[which]
        return remote(
            buffer.at[NBACK], buffer.at[NBACK - d], halo_sems, (which, d - 1), tok=lax.rem(t + d, ntok)
        )

    def head_share(d):
        return remote(sq_in.at[0], sq_in.at[d], head_sems, (d - 1,), head=lax.rem(h + d, nhead))

    def send_halo(which, *distances):
        for d in distances:
            halo(which, d).start()

    def swiglu(i):
        p1 = pre[aligned(i, 32), :]
        p3 = pre[pl.ds(pl.multiple_of(hid + i * 32, 32), 32), :]
        return p1 * sigmoid(p1) * p3

    def gradients(r):
        pre[...] = dot_nt(weights[r, 0 : 2 * hid, :], k_ref[...])
        back[0:hid, :] = dot_nt(weights[r, 2 * hid : 3 * hid, :], v_ref[...])
        mask = (ids[NBACK, 1:2, :] == r).astype(F32)

        @pl.loop(0, hid // 32)
        def _(i):
            p1 = pre[aligned(i, 32), :]
            p3 = pre[pl.ds(pl.multiple_of(hid + i * 32, 32), 32), :]
            b = back[aligned(i, 32), :] * mask
            s1 = sigmoid(p1)
            silu = p1 * s1
            delta[aligned(i, 32), :] = (-b * p3 * s1 * (1.0 + p1 * (1.0 - s1))).astype(BF16)
            delta[pl.ds(pl.multiple_of(hid + i * 32, 32), 32), :] = (-b * silu).astype(BF16)
            delta[pl.ds(pl.multiple_of(2 * hid + i * 32, 32), 32), :] = (-silu * p3 * mask).astype(BF16)

        if r == 0:
            pl.semaphore_wait(barrier, (NY - 1) + (nz - 1) + NBACK + (nhead - 1))
        for c in range(2):
            grad_send, grad_own = chunks[c][0], chunks[c][2]
            height = heights[c]
            for d in (1, 3, 2, 0):
                p = lax.rem(y + d, NY)
                here = pl.ds(pl.multiple_of(starts[c] + p * height, height), height)
                grad = dot_nn(delta[here, :], (k_ref, v_ref)[c][...])
                for j in range(cols):
                    part = grad[:, j * 128 : (j + 1) * 128]
                    if d:
                        grad_send[r, p, j * height : (j + 1) * height, :] = part.astype(BF16)
                    else:
                        grad_own[j * height : (j + 1) * height, :] = part
                if d:
                    y_scatter(r, c, d).start()

    def scatter_z(r, c):
        y_in, grad_own, z_out, z_own = chunks[c][1:5]
        for d in range(1, NY):
            y_scatter(r, c, d).wait_recv()

        def total(n):
            own = grad_own[aligned(n, blocks[c]), :]
            for d in range(1, NY):
                own = own + y_in[r, d - 1, aligned(n, blocks[c]), :].astype(F32)
            return own

        @pl.loop(1, nz)
        def _(d):
            z_out[r, aligned(lax.rem(z + d, nz), blocks[c]), :] = total(lax.rem(z + d, nz)).astype(BF16)
            z_scatter(r, c, d).start()

        z_own[...] = total(z)

    def gather_z(r, c):
        z_own, z_in, gathered = chunks[c][4:7]

        def add(d, total):
            z_scatter(r, c, d).wait_recv()
            return total + z_in[r, d - 1].astype(F32)

        total = lax.fori_loop(1, nz, add, z_own[...])
        gathered[r, y, aligned(z, blocks[c]), :] = total.astype(BF16)

        @pl.loop(1, nz)
        def _(d):
            z_gather(r, c, d, z).start()

    def gather_y(r, c):
        @pl.loop(1, nz)
        def _(d):
            z_gather(r, c, d, lax.rem(z + nz - d, nz)).wait_recv()

        for d in (1, 3, 2):
            y_gather(r, c, d, y).start()

    def finish_y(r, c):
        for d in range(1, NY):
            y_gather(r, c, d, lax.rem(y + NY - d, NY)).wait_recv()

    def step_scale(r, c, owners):
        gathered = chunks[c][6]
        total = jnp.zeros((8, 128), F32)
        for p in owners:
            for j in range(cols):
                x = gathered[r, p, j * heights[c] : (j + 1) * heights[c], :].astype(F32)
                total = total + jnp.sum((x * x).reshape(-1, 8, 128), axis=0)
        mean = jnp.sum(total, axis=(0, 1), keepdims=True) / float(hid * dh)
        return rate_ref[...] * lax.rsqrt(mean + EPSILON)

    def update(r, c):
        gathered = chunks[c][6]
        height = heights[c]
        parts = ((0, 1), (2, 3)) if c == 0 else ((0, 1, 2, 3),)
        for owners in parts:
            scale = step_scale(r, c, owners)
            for p in owners:
                for j in range(cols):
                    here = slice(starts[c] + p * height, starts[c] + (p + 1) * height)
                    lanes = slice(j * 128, (j + 1) * 128)
                    grad = gathered[r, p, j * height : (j + 1) * height, :].astype(F32)
                    weights[r + 1, here, lanes] = (
                        weights[r, here, lanes].astype(F32) - grad * scale
                    ).astype(BF16)

    def attend():
        wait_keys(False)

        @pl.loop(0, NBACK + 1)
        def _(s):
            scores[s] = dot_nt(q_ref[...], aall[s])

        mark = jnp.broadcast_to(ids[NBACK, 0:1, :].astype(F32), (128, rows)).T
        back[0:rows, 0:128] = mark

        @pl.loop(0, rows // 16)
        def _(i):
            here = aligned(i, 16)
            query_mark = back[here, 0:1] - 1.0
            query_at = t * rows + i * 16 + lax.broadcasted_iota(jnp.int32, (16, rows), 0)
            parts = []
            for s in range(NBACK + 1):
                key_at = (t - NBACK + s) * rows + lax.broadcasted_iota(jnp.int32, (16, rows), 1)
                allowed = (
                    (key_at <= query_at) & (key_at >= 0) & (ids[s, 0:1, :].astype(F32) >= query_mark)
                )
                parts.append(jnp.where(allowed, scores[s, here, :] * (1.0 / math.sqrt(dh)), -1e30))
            top = parts[0]
            for part in parts[1:]:
                top = jnp.maximum(top, part)
            top = jnp.max(top, axis=1, keepdims=True)
            parts = [jnp.exp(part - top) for part in parts]
            whole = parts[0]
            for part in parts[1:]:
                whole = whole + part
            inverse = 1.0 / jnp.sum(whole, axis=1, keepdims=True)
            for s in range(NBACK + 1):
                probs[s, here, :] = (parts[s] * inverse).astype(BF16)

    def apply_first():
        w2t[0] = weights[1, 2 * hid : 3 * hid, :].T
        pre[...] = dot_nt(weights[1, 0 : 2 * hid, :], q_ref[...])

        @pl.loop(0, hid // 32)
        def _(i):
            hidden_first[aligned(i, 32), :] = swiglu(i).astype(BF16)

    def apply_second():
        pre[...] = dot_nt(weights[2, 0 : 2 * hid, :], q_ref[...])
        first = ids[NBACK, 1:2, :] == 0

        @pl.loop(0, hid // 32)
        def _(i):
            here = aligned(i, 32)
            own = hidden_first[here, :].astype(F32)
            hidden[NBACK, here, :] = jnp.where(first, own, swiglu(i)).astype(BF16)

    def project(s):
        fast[...] = dot_nn(w2t[0], hidden[s])
        pre[...] = dot_nn(w2t[1], hidden[s])

    def mixed_rows(s, i):
        here = aligned(i, 32)
        return jnp.where(ids[s, 1:2, :] == 0, fast[here, :], pre[here, :])

    def share_norm():
        def add(i, total):
            x = mixed_rows(NBACK, i)
            return total + jnp.sum((x * x).reshape(4, 8, rows), axis=0)

        total = lax.fori_loop(0, dh // 32, add, jnp.zeros((8, rows), F32))
        total = jnp.sum(total, axis=0, keepdims=True)
        for j in range(rows // 128):
            sq_in[0, j : j + 1, :] = total[:, j * 128 : (j + 1) * 128]
        for d in range(1, nhead):
            head_share(d).start()
        for d in range(1, nhead):
            head_share(d).wait_recv()
        total = sq_in[0]
        for d in range(1, nhead):
            total = total + sq_in[d]
        norms[NBACK] = lax.rsqrt(total / float(nhead * dh) + EPSILON)

    def mix(s):
        norm = jnp.concatenate([norms[s, j : j + 1, :] for j in range(rows // 128)], axis=1)

        @pl.loop(0, dh // 32)
        def _(i):
            delta[aligned(i, 32), :] = (mixed_rows(s, i) * norm).astype(BF16)

        product = dot_nt(probs[s], delta[0:dh, :])
        if s == NBACK:
            back[...] = product
        else:
            back[...] = back[...] + product

    load_a.wait()
    gradients(0)
    send_halo(0, 1, 2, 3)
    scatter_z(0, 0)
    send_keys(0, 3)
    scatter_z(0, 1)
    send_keys(3, 6)
    gather_z(0, 0)
    send_keys(6, 9)
    gather_z(0, 1)
    send_keys(9, 12)
    gather_y(0, 0)
    gather_y(0, 1)
    finish_y(0, 0)
    update(0, 0)
    finish_y(0, 1)
    update(0, 1)
    send_keys(12, 15)
    gradients(1)
    for d in range(1, NBACK + 1):
        halo(0, d).wait_recv()
    scatter_z(1, 0)
    send_keys(15, 18)
    scatter_z(1, 1)
    send_keys(18, 21)
    apply_first()
    gather_z(1, 0)
    send_keys(21, 24)
    gather_z(1, 1)
    attend()
    gather_y(1, 0)
    gather_y(1, 1)
    finish_y(1, 0)
    update(1, 0)
    apply_second()
    send_halo(1, 1, 3, 2)
    finish_y(1, 1)
    update(1, 1)
    w2t[1] = weights[2, 2 * hid : 3 * hid, :].T
    project(NBACK)
    share_norm()
    send_halo(2, 1, 3, 2)
    mix(NBACK)
    for d in (1, 3, 2):
        halo(1, d).wait_recv()
        project(NBACK - d)
        halo(2, d).wait_recv()
        mix(NBACK - d)
    out_ref[...] = (back[...] * gain_ref[...].reshape(1, dh)).astype(BF16)
    wait_keys(True)
    for r in range(2):
        for c in range(2):
            for d in range(1, NY):
                y_scatter(r, c, d).wait_send()
                y_gather(r, c, d, y).wait_send()

            @pl.loop(1, nz)
            def _(d):
                z_scatter(r, c, d).wait_send()
                z_gather(r, c, d, z).wait_send()
    for which in range(3):
        for d in range(1, NBACK + 1):
            halo(which, d).wait_send()
    for d in range(1, nhead):
        head_share(d).wait_send()


def shards(queries, keys_fast, values_fast, keys_attn, w_one, w_three, w_two, step_size, norm_gain, group_ids, window_ids):
    rows, dh = queries.shape
    hid = w_one.shape[2]
    nz = lax.axis_size("tok") // NY
    nhead = lax.axis_size("head")
    dma = pltpu.SemaphoreType.DMA
    vmem = pl.BlockSpec(memory_space=pltpu.VMEM)
    anywhere = pl.BlockSpec(memory_space=pl.ANY)

    def chunk(height):
        piece = height // NY * (dh // 128)
        block = piece // nz
        return (
            pltpu.VMEM((2, NY, piece, 128), BF16),
            pltpu.VMEM((2, NY - 1, piece, 128), BF16),
            pltpu.VMEM((piece, 128), F32),
            pltpu.VMEM((2, piece, 128), BF16),
            pltpu.VMEM((block, 128), F32),
            pltpu.VMEM((2, nz - 1, block, 128), BF16),
            pltpu.VMEM((2, NY, piece, 128), BF16),
            dma((2, 2, NY - 1)),
            dma((2, 2, nz - 1)),
            dma((2, 2, nz - 1)),
            dma((2, 2, NY - 1)),
        )

    return pl.pallas_call(
        functools.partial(kernel, (nz, nhead, rows, dh, hid)),
        out_shape=jax.ShapeDtypeStruct((rows, dh), BF16),
        in_specs=[vmem] * 10 + [anywhere],
        out_specs=vmem,
        scratch_shapes=[
            pltpu.VMEM((NBACK + 1, rows, dh), BF16),
            pltpu.VMEM((NBACK + 1, 8, rows), jnp.int32),
            pltpu.VMEM((2 * hid, rows), F32),
            pltpu.VMEM((rows, rows), F32),
            pltpu.VMEM((3 * hid, rows), BF16),
            pltpu.VMEM((3, 3 * hid, dh), BF16),
            pltpu.VMEM((2, dh, hid), BF16),
            pltpu.VMEM((NBACK + 1, rows, rows), F32),
            pltpu.VMEM((NBACK + 1, rows, rows), BF16),
            pltpu.VMEM((hid, rows), BF16),
            pltpu.VMEM((NBACK + 1, hid, rows), BF16),
            pltpu.VMEM((dh, rows), F32),
            pltpu.VMEM((NBACK + 1, rows // 128, 128), F32),
            pltpu.VMEM((nhead, rows // 128, 128), F32),
            dma(()),
            dma((2, 3, NBACK)),
            dma((2, nhead - 1)),
            dma((2, NBACK, KEY_PARTS)),
            chunk(2 * hid),
            chunk(hid),
        ],
        compiler_params=pltpu.CompilerParams(
            collective_id=0, has_side_effects=True, vmem_limit_bytes=56 * 1024 * 1024
        ),
        name="fast_weight_attention",
    )(
        keys_fast,
        values_fast,
        w_one,
        w_three,
        w_two,
        step_size.reshape(1, 1),
        norm_gain,
        group_ids,
        window_ids,
        queries,
        keys_attn,
    )


def solution(mesh):
    in_specs = (
        P("tok", "head"),
        P("tok", "head"),
        P("tok", "head"),
        P("tok", "head"),
        P("head", None, None),
        P("head", None, None),
        P("head", None, None),
        P("head"),
        P("head"),
        P("tok"),
        P("tok"),
    )
    return jax.shard_map(shards, mesh=mesh, in_specs=in_specs, out_specs=P("tok", "head"), check_vma=False)
```

time: 206 us -> 147 us (0.71)
  the two profiles are of different devices: /device:TPU:6 before, /device:TPU:8 now
where the time goes in v2:
time: 147 us
  Pallas kernels  144 us (98%)
  local copies, waits for them, and re-layouts  1.87 us (1%)
    pallas_call x1, Pallas kernels, shards(): pl.pallas_call(functools.partial(kernel, (nz, nhead, rows, dh, hid)), out...  144 us

profile of v2, /device:TPU:8, one launch (start us, length us, event | category | flops | bytes accessed | tf_op | source)
XLA Modules:
  0.0 146.7 jit_solution(9052935605386052991)
XLA Ops:
  0.7 144.2 %fast_weight_attention.1 = bf16[512,512]{1,0:T(8,128)(2,1)} custom-call(bf16[512,512]{1,0:T(8,128)(2,1)} %k_ref.1, bf16[512,512]{1,0:T(8,128)(2,1)} %v_ref.1, bf16[1,512,256]{2,1,0:T(8,128)(2,1)} %w1_ref.1, bf16[1,512,256]{2,1,0:T(8,128)(2,1)} %w3_ref.1, bf16[1,256,512]{2,1,0:T(8,128)(2,1)} %w2_ref.1, f32[1,1]{1,0:T(1,128)} %bitcast.1.rate_ref, ...), custom_call_target="tpu_custom_call" | custom-call | tf_op jit(solution)/shard_map/fast_weight_attention/pallas_call | solution.py:484
  144.8 1.9 %copy.14 = bf16[512,512]{1,0:T(8,128)(2,1)} copy(bf16[512,512]{1,0:T(8,128)(2,1)} %fast_weight_attention.1) | data formatting | bytes 1048576

commit v3 on v2

--- a/solution.py
+++ b/solution.py
@@ -83,6 +83,10 @@
     def y_peer(d):
         return z * NY + lax.rem(y + d, NY)
 
+    def far_first(i):
+        half = lax.div(i + 1, 2)
+        return nz // 2 + half * (1 - 2 * lax.rem(i, 2))
+
     def z_peer(d):
         return lax.rem(z + d, nz) * NY + y
 
@@ -239,8 +243,9 @@
                 own = own + y_in[r, d - 1, aligned(n, blocks[c]), :].astype(F32)
             return own
 
-        @pl.loop(1, nz)
-        def _(d):
+        @pl.loop(0, nz - 1)
+        def _(i):
+            d = far_first(i)
             z_out[r, aligned(lax.rem(z + d, nz), blocks[c]), :] = total(lax.rem(z + d, nz)).astype(BF16)
             z_scatter(r, c, d).start()
 
@@ -256,9 +261,9 @@
         total = lax.fori_loop(1, nz, add, z_own[...])
         gathered[r, y, aligned(z, blocks[c]), :] = total.astype(BF16)
 
-        @pl.loop(1, nz)
-        def _(d):
-            z_gather(r, c, d, z).start()
+        @pl.loop(0, nz - 1)
+        def _(i):
+            z_gather(r, c, far_first(i), z).start()
 
     def gather_y(r, c):
         @pl.loop(1, nz)
@@ -390,36 +395,36 @@
 
     load_a.wait()
     gradients(0)
+    send_keys(0, 3)
     send_halo(0, 1, 2, 3)
     scatter_z(0, 0)
-    send_keys(0, 3)
+    send_keys(3, 6)
     scatter_z(0, 1)
-    send_keys(3, 6)
+    send_keys(6, 9)
     gather_z(0, 0)
-    send_keys(6, 9)
+    send_keys(9, 12)
     gather_z(0, 1)
-    send_keys(9, 12)
+    send_keys(12, 15)
     gather_y(0, 0)
     gather_y(0, 1)
+    send_keys(15, 18)
     finish_y(0, 0)
     update(0, 0)
     finish_y(0, 1)
     update(0, 1)
-    send_keys(12, 15)
+    send_keys(18, 21)
     gradients(1)
     for d in range(1, NBACK + 1):
         halo(0, d).wait_recv()
     scatter_z(1, 0)
-    send_keys(15, 18)
+    send_keys(21, 24)
     scatter_z(1, 1)
-    send_keys(18, 21)
     apply_first()
     gather_z(1, 0)
-    send_keys(21, 24)
     gather_z(1, 1)
-    attend()
     gather_y(1, 0)
     gather_y(1, 1)
+    attend()
     finish_y(1, 0)
     update(1, 0)
     apply_second()
@@ -437,6 +442,7 @@
         halo(2, d).wait_recv()
         mix(NBACK - d)
     out_ref[...] = (back[...] * gain_ref[...].reshape(1, dh)).astype(BF16)
+
     wait_keys(True)
     for r in range(2):
         for c in range(2):
@@ -448,6 +454,7 @@
             def _(d):
                 z_scatter(r, c, d).wait_send()
                 z_gather(r, c, d, z).wait_send()
+
     for which in range(3):
         for d in range(1, NBACK + 1):
             halo(which, d).wait_send()

time: 147 us -> 138 us (0.939)
  the two profiles are of different devices: /device:TPU:8 before, /device:TPU:6 now
where the time goes in v3:
time: 138 us
  Pallas kernels  135 us (98%)
  local copies, waits for them, and re-layouts  1.87 us (1%)
    pallas_call x1, Pallas kernels, shards(): pl.pallas_call(functools.partial(kernel, (nz, nhead, rows, dh, hid)), out...  135 us

profile of v3, /device:TPU:6, one launch (start us, length us, event | category | flops | bytes accessed | tf_op | source)
XLA Modules:
  0.0 137.8 jit_solution(5120933161854157022)
XLA Ops:
  0.7 135.3 %fast_weight_attention.1 = bf16[512,512]{1,0:T(8,128)(2,1)} custom-call(bf16[512,512]{1,0:T(8,128)(2,1)} %k_ref.1, bf16[512,512]{1,0:T(8,128)(2,1)} %v_ref.1, bf16[1,512,256]{2,1,0:T(8,128)(2,1)} %w1_ref.1, bf16[1,512,256]{2,1,0:T(8,128)(2,1)} %w3_ref.1, bf16[1,256,512]{2,1,0:T(8,128)(2,1)} %w2_ref.1, f32[1,1]{1,0:T(1,128)} %bitcast.1.rate_ref, ...), custom_call_target="tpu_custom_call" | custom-call | tf_op jit(solution)/shard_map/fast_weight_attention/pallas_call | solution.py:491
  136.0 1.9 %copy.14 = bf16[512,512]{1,0:T(8,128)(2,1)} copy(bf16[512,512]{1,0:T(8,128)(2,1)} %fast_weight_attention.1) | data formatting | bytes 1048576

commit v4 on v3

--- a/solution.py
+++ b/solution.py
@@ -219,7 +219,7 @@
         for c in range(2):
             grad_send, grad_own = chunks[c][0], chunks[c][2]
             height = heights[c]
-            for d in (1, 3, 2, 0):
+            for d in (2, 1, 3, 0):
                 p = lax.rem(y + d, NY)
                 here = pl.ds(pl.multiple_of(starts[c] + p * height, height), height)
                 grad = dot_nn(delta[here, :], (k_ref, v_ref)[c][...])
@@ -270,7 +270,7 @@
         def _(d):
             z_gather(r, c, d, lax.rem(z + nz - d, nz)).wait_recv()
 
-        for d in (1, 3, 2):
+        for d in (2, 1, 3):
             y_gather(r, c, d, y).start()
 
     def finish_y(r, c):
@@ -428,7 +428,7 @@
     finish_y(1, 0)
     update(1, 0)
     apply_second()
-    send_halo(1, 1, 3, 2)
+    send_halo(1, 2, 1, 3)
     finish_y(1, 1)
     update(1, 1)
     w2t[1] = weights[2, 2 * hid : 3 * hid, :].T

time: 138 us -> 140 us (1.014)
  Pallas kernels: 135 us -> 138 us
    pallas_call x1, Pallas kernels: 135 us -> 138 us  [shards(): pl.pallas_call(functools.partial(kernel, (nz, nhead, rows, dh, hid)), out...]
where the time goes in v4:
time: 140 us
  Pallas kernels  138 us (99%)
  local copies, waits for them, and re-layouts  1.87 us (1%)
    pallas_call x1, Pallas kernels, shards(): pl.pallas_call(functools.partial(kernel, (nz, nhead, rows, dh, hid)), out...  138 us

profile of v4, /device:TPU:6, one launch (start us, length us, event | category | flops | bytes accessed | tf_op | source)
XLA Modules:
  0.0 140.1 jit_solution(5630233702880509783)
XLA Ops:
  0.7 137.5 %fast_weight_attention.1 = bf16[512,512]{1,0:T(8,128)(2,1)} custom-call(bf16[512,512]{1,0:T(8,128)(2,1)} %k_ref.1, bf16[512,512]{1,0:T(8,128)(2,1)} %v_ref.1, bf16[1,512,256]{2,1,0:T(8,128)(2,1)} %w1_ref.1, bf16[1,512,256]{2,1,0:T(8,128)(2,1)} %w3_ref.1, bf16[1,256,512]{2,1,0:T(8,128)(2,1)} %w2_ref.1, f32[1,1]{1,0:T(1,128)} %bitcast.1.rate_ref, ...), custom_call_target="tpu_custom_call" | custom-call | tf_op jit(solution)/shard_map/fast_weight_attention/pallas_call | solution.py:491
  138.2 1.9 %copy.14 = bf16[512,512]{1,0:T(8,128)(2,1)} copy(bf16[512,512]{1,0:T(8,128)(2,1)} %fast_weight_attention.1) | data formatting | bytes 1048576
